TPU v7x, 512 devices: a whole 4x8x8 slice. The times are simulated.
512 devices in a mesh: gx: 32 (over y, x), gy: 16 (over z, core).
Axes of the slice: x: 4, y: 8, z: 8, core: 2. Of those that a mesh axis runs over, the one named last changes fastest.
Arguments:
- panel: bfloat16 [32, 16, 2, 128, 1024], P('gx', 'gy'), may hold values from -0.5 to 0.5
- corner_panel: bfloat16 [32, 16, 2, 24, 128], P('gx', 'gy'), may hold values from -0.5 to 0.5
- interface_diag: float32 [32, 16, 2, 1024], P('gx', 'gy'), may hold values from 0.5 to 2
- coarse_diag: float32 [32, 512], P('gx'), may hold values from 0.5 to 2
- scaling: float32 [32, 16, 8, 128], P('gx', 'gy'), may hold values from 0.5 to 2
- dual_rhs: float32 [32, 16, 8, 128], P('gx', 'gy'), may hold values from -6 to 6
- block_map: int32 [32, 16, 2, 8], P('gx', 'gy'), may hold values from 0 to 39
- corner_map: int32 [32, 16, 2, 24], P('gx', 'gy'), may hold values from 0 to 511
- counts: int32 [32, 16], P('gx', 'gy'), may hold values from 1 to 2, as said below
Outputs:
- multipliers: float32 [32, 16, 8, 128], P('gx', 'gy')
- residual: float32 [32, 16, 8, 128], P('gx', 'gy')
Inputs may be any that keep to these rules, and one draw needn't show every extreme that they name: `counts`: every device holds one or more live subdomains in its first slots; some device has all 2 slots live and some has one.
All inputs are finite; a program needn't handle non-finite values.
Results may differ from a plain program's by a relative error of at most 0.0003.
Values sent between devices are 32-bit elements; how exact they have to be, the bound alone decides.
No kernel may reach another device: no remote copies, remote signals or barrier semaphores. Data moves between devices by JAX's collectives and lax.ppermute only.
A program may use at most 64 MiB of HBM per device.

v0:
```python
import jax
import jax.numpy as jnp
from jax import lax
from jax.sharding import PartitionSpec as P

ITERS = 3


def extended(block, sides, width):
    for axis, dim in sides:
        count = lax.axis_size(axis)
        forward = [(i, i + 1) for i in range(count - 1)]
        backward = [(target, source) for source, target in forward]
        low = lax.ppermute(
            lax.slice_in_dim(block, block.shape[dim] - width, None, axis=dim), axis, forward
        )
        high = lax.ppermute(lax.slice_in_dim(block, 0, width, axis=dim), axis, backward)
        block = jnp.concatenate([low, block, high], axis=dim)
    return block


def weighted_norm(residual, precond):
    return lax.psum(jnp.sum(residual * precond), ("gx", "gy"))


def shards(
    panel,
    corner_panel,
    interface_diag,
    coarse_diag,
    scaling,
    dual_rhs,
    block_map,
    corner_map,
    counts,
):
    highest = lax.Precision.HIGHEST
    slots = panel.shape[2]
    width = panel.shape[4]
    owned = scaling.shape[2]
    block_size = scaling.shape[3]
    blocks_sub = width // block_size
    coarse_size = coarse_diag.shape[1]
    live = (lax.iota(jnp.int32, slots) < counts[0, 0]).astype(jnp.float32)
    factors = panel[0, 0]
    corners = corner_panel[0, 0]
    schur = jnp.einsum("sni,snj->sij", factors, factors, preferred_element_type=jnp.float32)
    width_eye = (lax.iota(jnp.int32, width)[:, None] == lax.iota(jnp.int32, width)[None, :]).astype(
        jnp.float32
    )
    schur = schur + interface_diag[0, 0][:, :, None] * width_eye[None]
    coupling = jnp.einsum("scn,sni->sci", corners, factors, preferred_element_type=jnp.float32)
    corner_block = (
        jnp.einsum("scn,sdn->scd", corners, corners, preferred_element_type=jnp.float32)
        * live[:, None, None]
    )
    local_map = block_map[0, 0]
    signs = jnp.where(local_map < owned, 1.0, -1.0) * live[:, None]
    picker = (local_map[:, :, None] == lax.iota(jnp.int32, 5 * owned)[None, None, :]).astype(
        jnp.float32
    ) * signs[:, :, None]
    coarse_iota = lax.iota(jnp.int32, coarse_size)
    own_hot = (corner_map[0, 0][:, :, None] == coarse_iota[None, None, :]).astype(jnp.float32)
    spread = jnp.einsum("sco,scd->sod", own_hot, corner_block, precision=highest)
    assembled = lax.psum(jnp.einsum("sod,sdp->op", spread, own_hot, precision=highest), "gy")
    coarse_eye = (coarse_iota[:, None] == coarse_iota[None, :]).astype(jnp.float32)
    system = assembled + coarse_diag[0][:, None] * coarse_eye
    lower = jnp.linalg.cholesky(system)

    def operate(field):
        padded = extended(field, (("gx", 0), ("gy", 1)), 1)
        candidates = jnp.concatenate(
            [padded[1, 1], padded[2, 1], padded[0, 1], padded[1, 2], padded[1, 0]], axis=0
        )
        gathered = jnp.einsum("sbk,kc->sbc", picker, candidates, precision=highest).reshape(
            slots, width
        )
        result = jnp.einsum("sij,sj->si", schur, gathered, precision=highest)
        corner_values = (
            jnp.einsum("sci,si->sc", coupling, gathered, precision=highest) * live[:, None]
        )
        coarse_right = lax.psum(
            jnp.einsum("sco,sc->o", own_hot, corner_values, precision=highest), "gy"
        )
        coarse_sol = jax.scipy.linalg.cho_solve((lower, True), coarse_right)
        back_values = jnp.einsum("sco,o->sc", own_hot, coarse_sol, precision=highest)
        result = result + jnp.einsum("sci,sc->si", coupling, back_values, precision=highest)
        contrib = jnp.einsum(
            "sbk,sbc->kc", picker, result.reshape(slots, blocks_sub, block_size), precision=highest
        )
        outgoing = contrib[owned:].reshape(4, owned, block_size)[None, None]
        incoming = extended(outgoing, (("gx", 0), ("gy", 1)), 1)
        image = field[0, 0] + contrib[:owned]
        image = (
            image + incoming[0, 1, 0] + incoming[2, 1, 1] + incoming[1, 0, 2] + incoming[1, 2, 3]
        )
        return image[None, None]

    multipliers = jnp.zeros_like(dual_rhs)
    residual = dual_rhs
    direction = scaling * residual
    norm_now = weighted_norm(residual, direction)
    for sweep_index in range(ITERS):
        image = operate(direction)
        alpha = norm_now / lax.psum(jnp.sum(direction * image), ("gx", "gy"))
        multipliers = multipliers + alpha * direction
        residual = dual_rhs - operate(multipliers)
        precond = scaling * residual
        norm_next = weighted_norm(residual, precond)
        direction = precond + norm_next / norm_now * direction
        norm_now = norm_next
    return (multipliers, residual)


def solution(mesh):
    return jax.shard_map(
        shards,
        mesh=mesh,
        in_specs=(
            P("gx", "gy", None, None, None),
            P("gx", "gy", None, None, None),
            P("gx", "gy", None, None),
            P("gx", None),
            P("gx", "gy", None, None),
            P("gx", "gy", None, None),
            P("gx", "gy", None, None),
            P("gx", "gy", None, None),
            P("gx", "gy"),
        ),
        out_specs=(P("gx", "gy", None, None), P("gx", "gy", None, None)),
        check_vma=False,
    )
```

profile of v0, /device:TPU:225, one launch (start us, length us, event | category | flops | bytes accessed | tf_op | source)
XLA Modules:
  0.0 1205.7 jit_solution(11194242693486896263)
XLA Ops:
  41.8 23.0 %psum.93 = f32[512]{0:T(512)S(1)} all-reduce(f32[512]{0:T(512)S(1)} %bitcast.1267), channel_id=1, replica_groups=mesh['gx'=32,'gy'=16] {'gy'}, use_global_device_ids=true, to_apply=%region_11.12 | all-reduce | flops 512 | bytes 4096 | tf_op jit(solution)/shard_map/psum | solution.py:82
  64.8 9.6 fusion.440
  74.4 64.5 %all-reduce.4.cloned.1.call-done = f32[512,512]{0,1:T(8,128)} async-done(((f32[512,512]{0,1:T(8,128)}), f32[512,512]{0,1:T(8,128)}) %all-reduce.4.cloned.1.call-update) | async-done | bytes 1048592 | tf_op jit(solution)/shard_map/psum | solution.py:65
  142.0 11.7 cholesky.103
  153.9 9.8 custom-call.32
  164.5 11.7 cholesky.215
  176.3 10.2 custom-call.33
  187.6 11.7 cholesky.236
  199.5 9.8 custom-call.34
  210.1 11.9 cholesky.253
  226.6 10.5 while.12
  237.1 40.1 %custom-call.40 = f32[4,128,128]{1,2,0:T(8,128)S(1)} custom-call(f32[4,128,128]{2,1,0:T(8,128)} %get-tuple-element.41), custom_call_target="InvertDiagBlocksLowerTriangular" | custom-call | tf_op jit(solution)/shard_map/jit(_cho_solve)/triangular_solve | solution.py:85
  302.2 95.9 %all-reduce.1 = (f32[]{:T(128)}, f32[]{:T(128)}) all-reduce(f32[]{:T(128)} %get-tuple-element.72, f32[]{:T(128)} %get-tuple-element.71), channel_id=1, replica_groups=mesh['gx'=32,'gy'=16] {'gx','gy'}, use_global_device_ids=true, to_apply=%region_1.2 | all-reduce | flops 2 | bytes 16 | tf_op jit(solution)/shard_map/psum | solution.py:23
  429.0 23.0 %psum.95 = f32[512]{0:T(512)S(1)} all-reduce(f32[512]{0:T(512)S(1)} %bitcast.1268), channel_id=1, replica_groups=mesh['gx'=32,'gy'=16] {'gy'}, use_global_device_ids=true, to_apply=%region_14.16 | all-reduce | flops 512 | bytes 4096 | tf_op jit(solution)/shard_map/psum | solution.py:82
  481.4 95.9 %psum.96 = f32[]{:T(128)} all-reduce(f32[]{:T(128)} %get-tuple-element.93), channel_id=1, replica_groups=mesh['gx'=32,'gy'=16] {'gx','gy'}, use_global_device_ids=true, to_apply=%region_16.18 | all-reduce | flops 1 | bytes 8 | tf_op jit(solution)/shard_map/psum | solution.py:23
  598.6 9.4 fusion.446
  608.3 23.0 %psum.97 = f32[512]{0:T(512)S(1)} all-reduce(f32[512]{0:T(512)S(1)} %bitcast.1269), channel_id=1, replica_groups=mesh['gx'=32,'gy'=16] {'gy'}, use_global_device_ids=true, to_apply=%region_17.19 | all-reduce | flops 512 | bytes 4096 | tf_op jit(solution)/shard_map/psum | solution.py:82
  660.7 95.9 %psum.98 = f32[]{:T(128)} all-reduce(f32[]{:T(128)} %fusion.229), channel_id=1, replica_groups=mesh['gx'=32,'gy'=16] {'gx','gy'}, use_global_device_ids=true, to_apply=%region_19.21 | all-reduce | flops 1 | bytes 8 | tf_op jit(solution)/shard_map/psum | solution.py:105
  777.8 9.4 fusion.449
  787.5 23.0 %psum.99 = f32[512]{0:T(512)S(1)} all-reduce(f32[512]{0:T(512)S(1)} %bitcast.1270), channel_id=1, replica_groups=mesh['gx'=32,'gy'=16] {'gy'}, use_global_device_ids=true, to_apply=%region_20.22 | all-reduce | flops 512 | bytes 4096 | tf_op jit(solution)/shard_map/psum | solution.py:82
  839.9 96.1 %psum.100 = f32[]{:T(128)} all-reduce(f32[]{:T(128)} %get-tuple-element.87), channel_id=1, replica_groups=mesh['gx'=32,'gy'=16] {'gx','gy'}, use_global_device_ids=true, to_apply=%region_22.24 | all-reduce | flops 1 | bytes 8 | tf_op jit(solution)/shard_map/psum | solution.py:23
  966.9 23.0 %psum.101 = f32[512]{0:T(512)S(1)} all-reduce(f32[512]{0:T(512)S(1)} %bitcast.1271), channel_id=1, replica_groups=mesh['gx'=32,'gy'=16] {'gy'}, use_global_device_ids=true, to_apply=%region_23.25 | all-reduce | flops 512 | bytes 4096 | tf_op jit(solution)/shard_map/psum | solution.py:82
  1019.2 95.9 %psum.102 = f32[]{:T(128)} all-reduce(f32[]{:T(128)} %fusion.216), channel_id=1, replica_groups=mesh['gx'=32,'gy'=16] {'gx','gy'}, use_global_device_ids=true, to_apply=%region_25.27 | all-reduce | flops 1 | bytes 8 | tf_op jit(solution)/shard_map/psum | solution.py:105
  1146.0 23.0 %psum.103 = f32[512]{0:T(512)S(1)} all-reduce(f32[512]{0:T(512)S(1)} %bitcast.1272), channel_id=1, replica_groups=mesh['gx'=32,'gy'=16] {'gy'}, use_global_device_ids=true, to_apply=%region_26.28 | all-reduce | flops 512 | bytes 4096 | tf_op jit(solution)/shard_map/psum | solution.py:82
  (362 shorter events, 352.6 us)
Async XLA Ops:
  7.2 131.7 %all-reduce.4.cloned.1.call-start = ((), (), s32[]{:S(2)}) async-start(), calls=%async_computation | async-start | bytes 2097152 | tf_op jit(solution)/shard_map/psum | solution.py:65
  8.0 20.4 %collective-permute-start.1 = (f32[1,1,8,128]{3,2,1,0:T(8,128)S(1)}, f32[1,1,8,128]{3,2,1,0:T(8,128)S(1)}, u32[]{:S(2)}, u32[]{:S(2)}) collective-permute-start(f32[1,1,8,128]{3,2,1,0:T(8,128)S(1)} %get-tuple-element.98), channel_id=1, source_target_pairs={{0,16},{16,32},{32,48},{48,64},{64,80},{80,96},{96,112},{112,128},... | collective-permute-start | bytes 12296 | tf_op jit(solution)/shard_map/ppermute | solution.py:14
  11.1 17.3 %collective-permute-start = (f32[1,1,8,128]{3,2,1,0:T(8,128)S(1)}, f32[1,1,8,128]{3,2,1,0:T(8,128)S(1)}, u32[]{:S(2)}, u32[]{:S(2)}) collective-permute-start(f32[1,1,8,128]{3,2,1,0:T(8,128)S(1)} %get-tuple-element.98), channel_id=1, source_target_pairs={{16,0},{32,16},{48,32},{64,48},{80,64},{96,80},{112,96},{128,112},... | collective-permute-start | bytes 12296 | tf_op jit(solution)/shard_map/ppermute | solution.py:17
  28.4 12.6 %collective-permute-start.3 = (f32[3,1,8,128]{3,2,1,0:T(8,128)S(1)}, f32[3,1,8,128]{3,2,1,0:T(8,128)S(1)}, u32[]{:S(2)}, u32[]{:S(2)}) collective-permute-start(f32[3,1,8,128]{3,2,1,0:T(8,128)S(1)} %pad_maximum_fusion.6), channel_id=1, source_target_pairs={{0,1},{1,2},{2,3},{3,4},{4,5},{5,6},{6,7},{7,8},{8,9},{9,10},{10,1... | collective-permute-start | bytes 36872 | tf_op jit(solution)/shard_map/ppermute | solution.py:14
  399.5 8.6 collective-permute-start.9
  408.8 9.9 collective-permute-start.11
  455.8 9.2 collective-permute-start.13
  471.2 8.4 collective-permute-start.15
  578.6 8.6 collective-permute-start.17
  588.0 10.1 collective-permute-start.19
  635.2 9.2 collective-permute-start.21
  650.6 8.4 collective-permute-start.23
  758.0 8.6 collective-permute-start.25
  767.3 9.9 collective-permute-start.27
  814.3 9.2 collective-permute-start.29
  829.7 8.4 collective-permute-start.31
  937.3 8.6 collective-permute-start.33
  946.7 9.9 collective-permute-start.35
  993.7 9.2 collective-permute-start.37
  1009.1 8.4 collective-permute-start.39
  1116.5 8.6 collective-permute-start.41
  1125.8 9.9 collective-permute-start.43
  1172.8 9.2 collective-permute-start.45
  1188.2 8.4 collective-permute-start.47
  (32 other events, 828.6 us)
Sparse Core Ops, SparseCore 0:
  21.6 117.2 all-reduce.3
where the time goes:
time: 1210 us
  blocking collectives  618 us (51%)
  starting transfers between devices  189 us (16%)
  waiting for transfers between devices  138 us (11%)
  other arithmetic  128 us (11%)
  matrix products  95.8 us (8%)
  between operations  25.5 us (2%)
    psum x3, blocking collectives, weighted_norm(): return lax.psum(jnp.sum(residual * precond), ('gx', 'gy'))  288 us
    psum x2, blocking collectives, shards(): alpha = norm_now / lax.psum(jnp.sum(direction * image), ('gx', 'gy'))  192 us
    psum x6, blocking collectives, operate(): lax.psum(jnp.einsum('sco,sc->o', own_hot, corner_values, precision=highes...  138 us
    ppermute x24, starting transfers between devices, extended(): lax.ppermute(lax.slice_in_dim(block, 0, width, axis=dim), axis, backward)  96.5 us
    ppermute x24, starting transfers between devices, extended(): lax.ppermute(lax.slice_in_dim(block, block.shape[dim] - width, None, axis...  92.8 us
    another operation x14, other arithmetic, shards(): lower = jnp.linalg.cholesky(system)  78.8 us
    psum x1, waiting for transfers between devices, shards(): lax.psum(jnp.einsum('sod,sdp->op', spread, own_hot, precision=highest), '...  64.5 us
    dot_general x6, matrix products, operate(): result = jnp.einsum('sij,sj->si', schur, gathered, precision=highest)  56.7 us
  transfers between devices with their start and end apart: 49, of which 24 were waited for; matrix products, arithmetic and copies ran while one was open for 2% of the time, Pallas kernels for 0%

commit v1 on v0

--- a/solution.py
+++ b/solution.py
@@ -62,7 +62,9 @@
     coarse_iota = lax.iota(jnp.int32, coarse_size)
     own_hot = (corner_map[0, 0][:, :, None] == coarse_iota[None, None, :]).astype(jnp.float32)
     spread = jnp.einsum("sco,scd->sod", own_hot, corner_block, precision=highest)
-    assembled = lax.psum(jnp.einsum("sod,sdp->op", spread, own_hot, precision=highest), "gy")
+    block_2 = jnp.einsum("sod,sdp->op", spread, own_hot, precision=highest)
+    terms = lax.all_gather(block_2, "gy")
+    assembled = jnp.sum(terms, axis=0)
     coarse_eye = (coarse_iota[:, None] == coarse_iota[None, :]).astype(jnp.float32)
     system = assembled + coarse_diag[0][:, None] * coarse_eye
     lower = jnp.linalg.cholesky(system)

time: 1210 us -> 1190 us (0.983)
  the two profiles are of different devices: /device:TPU:225 before, /device:TPU:223 now
where the time goes in v1:
time: 1190 us; the launch traced here: 1180 us
  blocking collectives  608 us (51%)
  starting transfers between devices  198 us (17%)
  other arithmetic  133 us (11%)
  waiting for transfers between devices  110 us (9%)
  matrix products  99.6 us (8%)
  between operations  25.5 us (2%)
    psum x3, blocking collectives, weighted_norm(): return lax.psum(jnp.sum(residual * precond), ('gx', 'gy'))  278 us
    psum x2, blocking collectives, shards(): alpha = norm_now / lax.psum(jnp.sum(direction * image), ('gx', 'gy'))  186 us
    psum x6, blocking collectives, operate(): lax.psum(jnp.einsum('sco,sc->o', own_hot, corner_values, precision=highes...  144 us
    ppermute x24, starting transfers between devices, extended(): lax.ppermute(lax.slice_in_dim(block, block.shape[dim] - width, None, axis...  137 us
    another operation x14, other arithmetic, shards(): lower = jnp.linalg.cholesky(system)  79.1 us
    ppermute x24, waiting for transfers between devices, extended(): lax.ppermute(lax.slice_in_dim(block, 0, width, axis=dim), axis, backward)  63.3 us
    ppermute x24, starting transfers between devices, extended(): lax.ppermute(lax.slice_in_dim(block, 0, width, axis=dim), axis, backward)  60.9 us
    dot_general x6, matrix products, operate(): result = jnp.einsum('sij,sj->si', schur, gathered, precision=highest)  57.1 us
  transfers between devices with their start and end apart: 49, of which 24 were waited for; matrix products, arithmetic and copies ran while one was open for 2% of the time, Pallas kernels for 0%

profile of v1, /device:TPU:223, one launch (start us, length us, event | category | flops | bytes accessed | tf_op | source)
XLA Modules:
  0.0 1184.0 jit_solution(7218659849683364241)
XLA Ops:
  38.5 25.8 %psum.85 = f32[512]{0:T(512)S(1)} all-reduce(f32[512]{0:T(512)S(1)} %bitcast.1268), channel_id=1, replica_groups=mesh['gx'=32,'gy'=16] {'gy'}, use_global_device_ids=true, to_apply=%region_11.12 | all-reduce | flops 512 | bytes 4096 | tf_op jit(solution)/shard_map/psum | solution.py:84
  64.3 9.7 fusion.439
  74.0 38.9 %all-gather.3.cloned.1.call-done = f32[8192,512]{1,0:T(8,128)} async-done(((f32[512,512]{1,0:T(8,128)}), f32[8192,512]{1,0:T(8,128)}) %all-gather.3.cloned.1.call-update) | async-done | bytes 16777232 | tf_op jit(solution)/shard_map/all_gather | solution.py:66
  122.5 11.7 cholesky.103
  134.3 9.8 custom-call.32
  146.7 12.2 %cholesky.215 = f32[128,128]{1,0:T(8,128)S(1)} custom-call(f32[128,128]{1,0:T(8,128)S(1)} %cholesky.267), custom_call_target="Cholesky" | custom-call | tf_op jit(solution)/shard_map/jit(cholesky)/cholesky | solution.py:70
  158.9 9.8 custom-call.33
  170.3 11.7 cholesky.236
  182.8 9.8 custom-call.34
  194.0 11.9 %cholesky.253 = f32[128,128]{1,0:T(8,128)S(1)} custom-call(f32[128,128]{1,0:T(8,128)S(1)} %convolution_subtract_fusion.2), custom_call_target="Cholesky" | custom-call | tf_op jit(solution)/shard_map/jit(cholesky)/cholesky | solution.py:70
  218.5 39.3 %custom-call.40 = f32[4,128,128]{1,2,0:T(8,128)S(1)} custom-call(f32[4,128,128]{2,1,0:T(8,128)S(1)} %get-tuple-element.41), custom_call_target="InvertDiagBlocksLowerTriangular" | custom-call | tf_op jit(solution)/shard_map/jit(_cho_solve)/triangular_solve | solution.py:87
  285.0 92.8 %all-reduce.1 = (f32[]{:T(128)}, f32[]{:T(128)}) all-reduce(f32[]{:T(128)} %get-tuple-element.48, f32[]{:T(128)} %get-tuple-element.47), channel_id=1, replica_groups=mesh['gx'=32,'gy'=16] {'gx','gy'}, use_global_device_ids=true, to_apply=%region_1.2 | all-reduce | flops 2 | bytes 16 | tf_op jit(solution)/shard_map/psum | solution.py:23
  396.8 9.4 fusion.442
  406.8 23.8 %psum.87 = f32[512]{0:T(512)S(1)} all-reduce(f32[512]{0:T(512)S(1)} %bitcast.1269), channel_id=1, replica_groups=mesh['gx'=32,'gy'=16] {'gy'}, use_global_device_ids=true, to_apply=%region_14.16 | all-reduce | flops 512 | bytes 4096 | tf_op jit(solution)/shard_map/psum | solution.py:84
  463.5 92.8 %psum.88 = f32[]{:T(128)} all-reduce(f32[]{:T(128)} %get-tuple-element.69), channel_id=1, replica_groups=mesh['gx'=32,'gy'=16] {'gx','gy'}, use_global_device_ids=true, to_apply=%region_16.18 | all-reduce | flops 1 | bytes 8 | tf_op jit(solution)/shard_map/psum | solution.py:23
  585.2 23.6 %psum.89 = f32[512]{0:T(512)S(1)} all-reduce(f32[512]{0:T(512)S(1)} %bitcast.1270), channel_id=1, replica_groups=mesh['gx'=32,'gy'=16] {'gy'}, use_global_device_ids=true, to_apply=%region_17.19 | all-reduce | flops 512 | bytes 4096 | tf_op jit(solution)/shard_map/psum | solution.py:84
  641.7 92.8 %psum.90 = f32[]{:T(128)} all-reduce(f32[]{:T(128)} %fusion.228), channel_id=1, replica_groups=mesh['gx'=32,'gy'=16] {'gx','gy'}, use_global_device_ids=true, to_apply=%region_19.21 | all-reduce | flops 1 | bytes 8 | tf_op jit(solution)/shard_map/psum | solution.py:107
  753.5 9.8 fusion.448
  763.9 23.6 %psum.91 = f32[512]{0:T(512)S(1)} all-reduce(f32[512]{0:T(512)S(1)} %bitcast.1271), channel_id=1, replica_groups=mesh['gx'=32,'gy'=16] {'gy'}, use_global_device_ids=true, to_apply=%region_20.22 | all-reduce | flops 512 | bytes 4096 | tf_op jit(solution)/shard_map/psum | solution.py:84
  820.3 92.8 %psum.92 = f32[]{:T(128)} all-reduce(f32[]{:T(128)} %get-tuple-element.63), channel_id=1, replica_groups=mesh['gx'=32,'gy'=16] {'gx','gy'}, use_global_device_ids=true, to_apply=%region_22.24 | all-reduce | flops 1 | bytes 8 | tf_op jit(solution)/shard_map/psum | solution.py:23
  932.1 9.4 fusion.451
  942.1 23.6 %psum.93 = f32[512]{0:T(512)S(1)} all-reduce(f32[512]{0:T(512)S(1)} %bitcast.1272), channel_id=1, replica_groups=mesh['gx'=32,'gy'=16] {'gy'}, use_global_device_ids=true, to_apply=%region_23.25 | all-reduce | flops 512 | bytes 4096 | tf_op jit(solution)/shard_map/psum | solution.py:84
  998.6 93.0 %psum.94 = f32[]{:T(128)} all-reduce(f32[]{:T(128)} %fusion.215), channel_id=1, replica_groups=mesh['gx'=32,'gy'=16] {'gx','gy'}, use_global_device_ids=true, to_apply=%region_25.27 | all-reduce | flops 1 | bytes 8 | tf_op jit(solution)/shard_map/psum | solution.py:107
  1120.5 23.6 %psum.95 = f32[512]{0:T(512)S(1)} all-reduce(f32[512]{0:T(512)S(1)} %bitcast.1273), channel_id=1, replica_groups=mesh['gx'=32,'gy'=16] {'gy'}, use_global_device_ids=true, to_apply=%region_26.28 | all-reduce | flops 512 | bytes 4096 | tf_op jit(solution)/shard_map/psum | solution.py:84
  (347 shorter events, 365.5 us)
Async XLA Ops:
  7.2 105.7 %all-gather.3.cloned.1.call-start = ((), (), s32[]{:S(2)}) async-start(), calls=%async_computation | async-start | bytes 17825792 | tf_op jit(solution)/shard_map/all_gather | solution.py:66
  12.9 15.5 %collective-permute-start = (f32[1,1,8,128]{3,2,1,0:T(8,128)S(1)}, f32[1,1,8,128]{3,2,1,0:T(8,128)S(1)}, u32[]{:S(2)}, u32[]{:S(2)}) collective-permute-start(f32[1,1,8,128]{3,2,1,0:T(8,128)S(1)} %get-tuple-element.74), channel_id=1, source_target_pairs={{16,0},{32,16},{48,32},{64,48},{80,64},{96,80},{112,96},{128,112},... | collective-permute-start | bytes 12296 | tf_op jit(solution)/shard_map/ppermute | solution.py:17
  15.4 13.1 %collective-permute-start.1 = (f32[1,1,8,128]{3,2,1,0:T(8,128)S(1)}, f32[1,1,8,128]{3,2,1,0:T(8,128)S(1)}, u32[]{:S(2)}, u32[]{:S(2)}) collective-permute-start(f32[1,1,8,128]{3,2,1,0:T(8,128)S(1)} %get-tuple-element.74), channel_id=1, source_target_pairs={{0,16},{16,32},{32,48},{48,64},{64,80},{80,96},{96,112},{112,128},... | collective-permute-start | bytes 12296 | tf_op jit(solution)/shard_map/ppermute | solution.py:14
  28.5 8.5 collective-permute-start.2
  266.0 7.8 collective-permute-start.5
  379.2 8.6 collective-permute-start.8
  434.4 9.2 collective-permute-start.12
  441.6 7.8 collective-permute-start.13
  449.4 8.8 collective-permute-start.14
  557.6 8.6 collective-permute-start.16
  612.6 9.2 collective-permute-start.20
  619.9 7.8 collective-permute-start.21
  627.7 8.8 collective-permute-start.22
  735.9 8.6 collective-permute-start.24
  791.3 9.2 collective-permute-start.28
  798.5 7.8 collective-permute-start.29
  806.3 8.8 collective-permute-start.30
  914.5 8.6 collective-permute-start.32
  969.5 9.2 collective-permute-start.36
  976.7 7.8 collective-permute-start.37
  984.5 8.8 collective-permute-start.38
  1092.9 8.6 collective-permute-start.40
  1147.9 9.2 collective-permute-start.44
  1163.0 8.8 collective-permute-start.46
  (33 other events, 750.2 us)
Sparse Core Ops, SparseCore 0:
  12.3 100.5 all-gather.2
